TPU v7x, 32 devices: a whole 2x2x4 slice. The times are simulated.
32 devices in a mesh: pipe: 4 (over y, x), dp: 8 (over z, core).
Axes of the slice: x: 2, y: 2, z: 4, core: 2. Of those that a mesh axis runs over, the one named last changes fastest.
Arguments:
- inputs: bfloat16 [4, 16, 784, 384], P(None, 'dp'), may hold values from -6 to 6
- cotangent: bfloat16 [4, 16, 784, 384], P(None, 'dp'), may hold values from -6 to 6
- pad_mask: int32 [4, 16, 784], P(None, 'dp'), may hold values from 0 to 1, as said below
- region_ids: int32 [4, 16, 784], P(None, 'dp'), may hold values from 0 to 35, as said below
- norm1_gain: float32 [2, 384], P(None, 'dp'), may hold values from 0.5 to 1.5
- norm1_bias: float32 [2, 384], P(None, 'dp'), may hold values from -1.5 to 1.5
- qkv_weight: float32 [2, 384, 1152], P(None, 'dp'), may hold values from -0.3125 to 0.3125
- qv_bias: float32 [2, 768], P(None, 'dp'), may hold values from -3 to 3
- rel_table: float32 [2, 169, 12], replicated, may hold values from -4 to 4
- proj_weight: float32 [2, 384, 384], P(None, 'dp'), may hold values from -0.875 to 0.875
- proj_bias: float32 [2, 384], P(None, 'dp'), may hold values from -1.5 to 1.5
- norm2_gain: float32 [2, 384], P(None, 'dp'), may hold values from 0.5 to 1.5
- norm2_bias: float32 [2, 384], P(None, 'dp'), may hold values from -1.5 to 1.5
- fc1_weight: float32 [2, 384, 1536], P(None, 'dp'), may hold values from -0.3125 to 0.3125
- fc1_bias: float32 [2, 1536], P(None, 'dp'), may hold values from -3 to 3
- fc2_weight: float32 [2, 1536, 384], P(None, 'dp'), may hold values from -0.21875 to 0.21875
- fc2_bias: float32 [2, 384], P(None, 'dp'), may hold values from -1.5 to 1.5
Outputs:
- activations: bfloat16 [4, 4, 16, 784, 384], P('pipe', None, 'dp')
- input_grads: bfloat16 [4, 4, 16, 784, 384], P('pipe', None, 'dp')
- grad_norm1_gain: float32 [2, 384], P(None, 'dp')
- grad_norm1_bias: float32 [2, 384], P(None, 'dp')
- grad_qkv_weight: float32 [2, 384, 1152], P(None, 'dp')
- grad_qv_bias: float32 [2, 768], P(None, 'dp')
- grad_rel_table: float32 [2, 169, 12], replicated
- grad_proj_weight: float32 [2, 384, 384], P(None, 'dp')
- grad_proj_bias: float32 [2, 384], P(None, 'dp')
- grad_norm2_gain: float32 [2, 384], P(None, 'dp')
- grad_norm2_bias: float32 [2, 384], P(None, 'dp')
- grad_fc1_weight: float32 [2, 384, 1536], P(None, 'dp')
- grad_fc1_bias: float32 [2, 1536], P(None, 'dp')
- grad_fc2_weight: float32 [2, 1536, 384], P(None, 'dp')
- grad_fc2_bias: float32 [2, 384], P(None, 'dp')
Inputs may be any that keep to these rules, and one draw needn't show every extreme that they name: `pad_mask`: 1 marks a cell of an image. A canvas holds either four equal square images, one in each quarter of the canvas, all real, or one image of 24 x 24 cells in its upper left corner with the rest padding. `region_ids`: cells of different images have different ids; within an image, cells share an id exactly when they lie in the same one of three bands of rows and of columns (the first 3, then up to 4 before the image's padded end, then the rest).
All inputs are finite; a program needn't handle non-finite values.
Results may differ from a plain program's by a relative error of at most 0.018.
Values may be sent and summed in bfloat16 or wider, within the bound.
A program may use at most 192 MiB of HBM per device.

v0:
```python
import functools
import types

import jax
import jax.numpy as jnp
import numpy as np
from jax import lax
from jax.experimental import pallas as pl
from jax.experimental.pallas import tpu as pltpu
from jax.sharding import PartitionSpec as P

HEADS = 12
WIN = 7
SHIFT = 3
GRID = 28
CELLS = 784
D = 384
FF = 1536
HEAD = 32
SIDE = 4
WINDOWS = 16
PLACES = 64
WROWS = WINDOWS * PLACES
GROUPS = 3
TILE = 112
SCALE = HEAD**-0.5
NORM_EPS = 1e-05
MASKED = -1e30
BF = jnp.bfloat16
F32 = jnp.float32

ERF_P = 0.3275911 / np.sqrt(2.0)
ERF_A = [0.5 * a for a in (0.254829592, -0.284496736, 1.421413741, -1.453152027, 1.061405429)]
PHI_0 = 1.0 / np.sqrt(2.0 * np.pi)


def nn(a, b):
    return lax.dot_general(a, b, (((1,), (0,)), ((), ())), preferred_element_type=F32)


def nt(a, b):
    return lax.dot_general(a, b, (((1,), (1,)), ((), ())), preferred_element_type=F32)


def tn(a, b):
    return lax.dot_general(a, b, (((0,), (0,)), ((), ())), preferred_element_type=F32)


def segments(shift):
    runs = []
    for wr in range(SIDE):
        for r in range(WIN):
            row = (wr * WIN + r + shift) % GRID
            for wc in range(SIDE):
                col = (wc * WIN + shift) % GRID
                place = (wr * SIDE + wc) * PLACES + r * 8
                first = min(WIN, GRID - col)
                runs.append((row * GRID + col, place, first))
                if first < WIN:
                    runs.append((row * GRID, place + first, WIN - first))
    return runs


def to_windows(src, dst, shift):
    for cell, place, count in segments(shift):
        dst[pl.ds(place, count), :] = src[pl.ds(cell, count), :]


def to_canvas(src, dst, shift):
    for cell, place, count in segments(shift):
        dst[pl.ds(cell, count), :] = src[pl.ds(place, count), :]


def row_block(t, size):
    return pl.ds(pl.multiple_of(t * size, 16), size)


def standardized(v):
    centered = v - jnp.mean(v, axis=-1, keepdims=True)
    spread = jnp.mean(centered * centered, axis=-1, keepdims=True)
    rs = lax.rsqrt(spread + NORM_EPS)
    return centered * rs, rs


def by_eights(v):
    return jnp.sum(v.reshape(v.shape[0] // 8, 8, v.shape[1]), axis=0)


def gelu_parts(x):
    den = 1.0 + ERF_P * jnp.abs(x)
    t = pl.reciprocal(den, approx=True)
    t = t * (2.0 - den * t)
    e = jnp.exp(-0.5 * x * x)
    poly = ERF_A[4]
    for a in ERF_A[3::-1]:
        poly = poly * t + a
    tail = poly * t * e
    cdf = jnp.where(x >= 0.0, 1.0 - tail, tail)
    return x * cdf, cdf + x * (e * PHI_0)


def real_places(rows):
    place = lax.broadcasted_iota(jnp.int32, (rows, 1), 0)
    return ((place & 7) < WIN) & (((place >> 3) & 7) < WIN)


def head_of_lane():
    return lax.broadcasted_iota(jnp.int32, (PLACES, 128), 1) >> 5


def by_head(x, lanes):
    zero = jnp.zeros_like(x)
    return jnp.concatenate([jnp.where(lanes == h, x, zero) for h in range(4)], axis=0)


def own_head(wide, lanes):
    out = wide[3 * PLACES :]
    for h in (2, 1, 0):
        out = jnp.where(lanes == h, wide[h * PLACES : (h + 1) * PLACES], out)
    return out


MESH = pl.DeviceIdType.MESH
ATT_ROWS = 256
MLP_ROWS = 384
SMALL = 192


def kernel(names, linked, canvases, *refs):
    r = types.SimpleNamespace(**dict(zip(names, refs)))
    me = lax.axis_index("pipe")
    inb, code, codew, buf = r.inb, r.code, r.codew, r.buf
    hqw, qkv, probs, att = r.hqw, r.qkv, r.probs, r.att
    hq2, hid, dgelu = r.hq2, r.hid, r.dgelu
    canvf, winf, gzw, wide_t, gqkv, go = r.canvf, r.winf, r.gzw, r.wide_t, r.gqkv, r.go
    g_qkv, g_proj, g_fc1, g_fc2t, g_vec, g_tab = r.g_qkv, r.g_proj, r.g_fc1, r.g_fc2t, r.g_vec, r.g_tab
    wat, fc1, fc2, vec, bias = r.wat, r.fc1, r.fc2, r.vec, r.bias
    if linked:
        d = lax.axis_index("dp")
        z, c = d // 2, d % 2
        sibling = {"dp": 2 * z + 1 - c}

    def z_peer(k):
        return {"dp": 2 * lax.rem(z + k, 4) + c}

    def pipe_peer(k):
        return {"pipe": lax.rem(me + k, 4)}

    def dp_peer(k):
        return {"dp": lax.rem(d + k, 8)}

    def remote(src, dst, send, recv, device):
        return pltpu.make_async_remote_copy(
            src_ref=src, dst_ref=dst, send_sem=send, recv_sem=recv, device_id=device, device_id_type=MESH
        )

    barrier = pltpu.get_barrier_semaphore()
    partners = [pipe_peer(k) for k in range(1, 4)]
    if linked:
        partners += [dp_peer(k) for k in range(1, 8)]
    for partner in partners:
        pl.semaphore_signal(barrier, inc=1, device_id=partner, device_id_type=MESH)

    full = ((wat,), (fc1, fc2), (wat,), (fc1, fc2))

    def owner_back(k):
        return 2 * lax.rem(z + 4 - k, 4) + c

    def shard(sec, a, owner):
        h = 192 if a else 48
        return full[sec][a].at[sec // 2, pl.ds(pl.multiple_of(owner * h, 16), h), :]

    def part(sec, a, owner, place):
        if a:
            return fc2.at[sec // 2, pl.ds(pl.multiple_of(owner * 192 + place * 48, 16), 48), :]
        rows = pl.ds(pl.multiple_of(owner * 48, 16), 48)
        return full[sec][0].at[sec // 2, rows, pl.ds(pl.multiple_of(place * D, 128), D)]

    def to_z(sec, a, k):
        own = part(sec, a, d, me)
        return remote(own, own, r.wz_send.at[sec, a, k - 1], r.wz_recv.at[sec, a, k - 1], z_peer(k))

    def to_places(sec, a, k, j):
        got = part(sec, a, owner_back(k), me)
        return remote(
            got, got, r.wx_send.at[sec, a, k - 1, j - 1], r.wx_recv.at[sec, a, k - 1, j - 1], pipe_peer(j)
        )

    def to_sibling(sec, a, k):
        block = shard(sec, a, owner_back(k))
        return remote(block, block, r.ws_send.at[sec, a, k], r.ws_recv.at[sec, a, k], sibling)

    def weights_1(sec):
        for a in range(len(full[sec])):
            for k in range(1, 4):
                to_z(sec, a, k).start()
            to_sibling(sec, a, 0).start()

    def weights_2(sec):
        for k in range(1, 4):
            for a in range(len(full[sec])):
                got = part(sec, a, owner_back(k), me)
                remote(got, got, r.wz_send.at[sec, a, k - 1], r.wz_recv.at[sec, a, k - 1], z_peer(k)).wait_recv()
                for j in range(1, 4):
                    to_places(sec, a, k, j).start()

    def weights_3(sec):
        for k in range(1, 4):
            for a in range(len(full[sec])):
                for j in range(1, 4):
                    got = part(sec, a, owner_back(k), lax.rem(me + 4 - j, 4))
                    remote(
                        got, got, r.wx_send.at[sec, a, k - 1, j - 1], r.wx_recv.at[sec, a, k - 1, j - 1], pipe_peer(j)
                    ).wait_recv()
                to_sibling(sec, a, k).start()

    def weights_4(sec):
        for k in range(4):
            for a in range(len(full[sec])):
                block = shard(sec, a, 2 * lax.rem(z + 4 - k, 4) + 1 - c)
                remote(block, block, r.ws_send.at[sec, a, k], r.ws_recv.at[sec, a, k], sibling).wait_recv()

    def weights_sent():
        for sec in range(4):
            for a in range(len(full[sec])):
                for k in range(4):
                    to_sibling(sec, a, k).wait_send()
                    if k:
                        to_z(sec, a, k).wait_send()
                        for j in range(1, 4):
                            to_places(sec, a, k, j).wait_send()

    def pack_copy(k):
        return remote(
            r.packs.at[d], r.packs.at[d], r.pk_send.at[k - 1], r.pk_recv.at[k - 1], dp_peer(k)
        )

    def pack_arrival(k):
        slot = r.packs.at[lax.rem(d + 8 - k, 8)]
        return remote(slot, slot, r.pk_send.at[k - 1], r.pk_recv.at[k - 1], dp_peer(k))

    def place_vectors():
        kind = lax.broadcasted_iota(jnp.int32, (16, 256), 0) & 7
        lane = lax.broadcasted_iota(jnp.int32, (16, 256), 1)
        vec[...] = jnp.zeros_like(vec)
        for width, kinds in ((48, kind < 6), (96, kind == 6), (192, kind == 7)):
            for owner in range(8):
                at = owner * width
                if width == 96 and owner >= 4:
                    at += D
                start = at // 128 * 128
                part = jnp.where(kinds & (lane < width), r.packs[owner].astype(F32), 0.0)
                if at > start:
                    part = pltpu.roll(part, at - start, 1)
                vec[:, start : start + 256] += part

    def pieces(sec, owner):
        b = sec // 2
        out = []

        def matrix(ref, h):
            for t in range(h // 48):
                rows = pl.ds(pl.multiple_of(owner * h + t * 48, 16), 48)
                for j in range(ref.shape[1] // D):
                    load = functools.partial(lambda ref, rows, j: ref[rows, j * D : (j + 1) * D], ref, rows, j)
                    out.append((len(out) * 48, 48, load))

        def small():
            rows = pl.ds(pl.multiple_of(owner * 8, 8), 8)
            parts = [g_tab[b, rows, j * D : (j + 1) * D] for j in range(2)]
            parts += [g_vec[b, owner, :, j * D : (j + 1) * D] for j in range(4)]
            return jnp.concatenate(parts + [jnp.zeros((16, D), F32)], axis=0)

        if sec % 2:
            matrix(g_fc1, 48)
        else:
            matrix(g_qkv, 48)
            matrix(g_proj, 48)
            out.append((SMALL, 64, small))
        return out

    def reduce_refs(sec):
        kind = "m" if sec % 2 else "a"
        return types.SimpleNamespace(
            **{n: getattr(r, kind + "_" + n) for n in ("st_a", "rc_a", "st_b", "rc_b", "st_c", "rc_c", "fin")}
        )

    def step_1(sec):
        q = reduce_refs(sec)
        if sec < 2:
            copy_a(sec + 2).wait_send()
            for k in range(1, 4):
                copy_b(sec + 2, k).wait_send()
                copy_c(sec + 2, k).wait_send()
        for k in range(4):
            i = lax.rem(z + k, 4)
            kept = q.st_b.at[k - 1] if k else q.st_c
            for row, rows, load in pieces(sec, 2 * i + 1 - c):
                q.st_a[i, row : row + rows, :] = load().astype(BF)
            for row, rows, load in pieces(sec, 2 * i + c):
                kept[row : row + rows, :] = load().astype(BF)
            if sec % 2:
                winf[:D, :] = g_fc2t[:, pl.ds(pl.multiple_of(i * D, 128), D)].T
                for t in range(0, 192, 48):
                    at = slice(192 + t, 240 + t)
                    q.st_a[i, at, :] = winf[pl.ds(pl.multiple_of((1 - c) * 192 + t, 16), 48), :].astype(BF)
                    kept[at, :] = winf[pl.ds(pl.multiple_of(c * 192 + t, 16), 48), :].astype(BF)
        copy_a(sec).start()

    def copy_a(sec):
        q = reduce_refs(sec)
        return remote(q.st_a, q.rc_a, r.ra_send.at[sec], r.ra_recv.at[sec], sibling)

    def copy_b(sec, k):
        q = reduce_refs(sec)
        return remote(
            q.st_b.at[k - 1], q.rc_b.at[k - 1], r.rb_send.at[sec, k - 1], r.rb_recv.at[sec, k - 1], z_peer(k)
        )

    def step_2(sec):
        q = reduce_refs(sec)
        copy_a(sec).wait_recv()
        for k in (1, 2, 3, 0):
            i = lax.rem(z + k, 4)
            kept = q.st_b.at[k - 1] if k else q.st_c
            for row in range(0, kept.shape[0], 64):
                at = slice(row, row + 64)
                kept[at, :] = (kept[at, :].astype(F32) + q.rc_a[i, at, :].astype(F32)).astype(BF)
            if k:
                copy_b(sec, k).start()

    def quarter(sec, ref, who):
        rows = (MLP_ROWS if sec % 2 else ATT_ROWS) // 4
        return ref.at[pl.ds(pl.multiple_of(who * rows, 16), rows), :]

    def copy_c(sec, k):
        q = reduce_refs(sec)
        return remote(
            quarter(sec, q.st_c, lax.rem(me + k, 4)),
            q.rc_c.at[k - 1],
            r.rc_send.at[sec, k - 1],
            r.rc_recv.at[sec, k - 1],
            pipe_peer(k),
        )

    def step_3(sec):
        q = reduce_refs(sec)
        for k in range(1, 4):
            copy_b(sec, k).wait_recv()
        for row in range(0, q.st_c.shape[0], 64):
            at = slice(row, row + 64)
            total = q.st_c[at, :].astype(F32)
            for k in range(3):
                total = total + q.rc_b[k, at, :].astype(F32)
            q.st_c[at, :] = total.astype(BF)
        for k in range(1, 4):
            copy_c(sec, k).start()

    def copy_f(sec, k):
        q = reduce_refs(sec)
        own = quarter(sec, q.fin, me)
        return remote(own, own, r.rf_send.at[sec, k - 1], r.rf_recv.at[sec, k - 1], pipe_peer(k))

    def step_4(sec):
        q = reduce_refs(sec)
        for k in range(1, 4):
            copy_c(sec, k).wait_recv()
            if sec < 2:
                copy_f(sec + 2, k).wait_send()
        total = quarter(sec, q.st_c, me)[...].astype(F32)
        for k in range(3):
            total = total + q.rc_c[k].astype(F32)
        quarter(sec, q.fin, me)[...] = total.astype(BF)
        for k in range(1, 4):
            copy_f(sec, k).start()

    def copy_s(b, k):
        rows = pl.ds(SMALL, 64)
        return remote(
            r.a_fin.at[rows, :], r.o_small.at[b, d], r.rs_send.at[b, k - 1], r.rs_recv.at[b, k - 1], dp_peer(k)
        )

    def own_small(b):
        return pltpu.make_async_copy(r.a_fin.at[pl.ds(SMALL, 64), :], r.o_small.at[b, d], r.os_sem.at[b])

    def outputs(sec):
        pairs = ((r.l_fc1, r.o_fc1), (r.l_fc2, r.o_fc2)) if sec % 2 else ((r.l_qkv, r.o_qkv), (r.l_proj, r.o_proj))
        return [
            pltpu.make_async_copy(ref, out.at[sec // 2], r.go_sem.at[sec, i]) for i, (ref, out) in enumerate(pairs)
        ]

    def step_5(sec):
        q = reduce_refs(sec)
        b = sec // 2
        for k in range(1, 4):
            got = quarter(sec, q.fin, lax.rem(me + 4 - k, 4))
            remote(got, got, r.rf_send.at[sec, k - 1], r.rf_recv.at[sec, k - 1], pipe_peer(k)).wait_recv()
        if sec % 2 == 0:
            for k in range(1, 8):
                copy_s(b, k).start()
            own_small(b).start()
        if sec < 2:
            for out in outputs(sec + 2):
                out.wait()
        row = 0
        for ref in (r.l_fc1, r.l_fc2) if sec % 2 else (r.l_qkv, r.l_proj):
            for t in range(ref.shape[0] // 48):
                for j in range(ref.shape[1] // D):
                    ref[t * 48 : (t + 1) * 48, j * D : (j + 1) * D] = q.fin[row : row + 48, :].astype(F32)
                    row += 48
        for out in outputs(sec):
            out.start()

    def smalls_sent(b):
        for k in range(1, 8):
            copy_s(b, k).wait_send()
        own_small(b).wait()

    def reductions_done():
        for sec in (1, 0):
            copy_a(sec).wait_send()
            for k in range(1, 4):
                copy_b(sec, k).wait_send()
                copy_c(sec, k).wait_send()
                copy_f(sec, k).wait_send()
        for sec in range(2):
            for out in outputs(sec):
                out.wait()
        smalls_sent(0)
        for b in range(2):
            for k in range(1, 8):
                rows = pl.ds(SMALL, 64)
                remote(
                    r.a_fin.at[rows, :],
                    r.o_small.at[b, lax.rem(d + 8 - k, 8)],
                    r.rs_send.at[b, k - 1],
                    r.rs_recv.at[b, k - 1],
                    dp_peer(k),
                ).wait_recv()

    if linked:
        lands = ((r.s_qkv, g_qkv, wat, 0), (r.s_proj, g_proj, wat, 3 * D), (r.s_fc1, g_fc1, fc1, 0), (r.s_fc2, g_fc2t, fc2, 0))

        def landing(i, b):
            src, dst, _, _ = lands[i]
            h, n = src.shape[1:]
            return pltpu.make_async_copy(
                src.at[b], dst.at[pl.ds(192 * b, h), pl.ds(0, n)], r.sh_sem.at[i, b]
            )

        for i in range(4):
            for b in range(2):
                landing(i, b).start()
        r.packs[d] = r.pack[...]
        for i, (src, dst, ref, col) in enumerate(lands):
            h, n = src.shape[1:]
            for b in range(2):
                landing(i, b).wait()
                for t in range(0, h, 48):
                    rows = pl.ds(pl.multiple_of(d * h + t, 16), 48)
                    ref[b, rows, col : col + n] = dst[192 * b + t : 192 * b + t + 48, :n].astype(BF)
    pl.semaphore_wait(barrier, len(partners))
    if linked:
        for k in range(1, 8):
            pack_copy(k).start()
        weights_1(0)

    def cleared(*refs):
        for ref in refs:

            @pl.loop(0, ref.shape[0] // 16)
            def _(i):
                ref[row_block(i, 16), :] = jnp.zeros((16, ref.shape[1]), F32)

    g_vec[...] = jnp.zeros_like(g_vec)
    g_tab[...] = jnp.zeros_like(g_tab)
    codew[...] = jnp.zeros_like(codew)

    if linked:
        weights_2(0)
        for sec in range(1, 4):
            weights_1(sec)
        for k in range(1, 8):
            pack_arrival(k).wait_recv()
        place_vectors()
        weights_3(0)
        weights_4(0)

    def vector(b, kind, width=D):
        return vec[b * 8 + kind : b * 8 + kind + 1, :width]

    def add_vec(b, kind, part):
        g_vec[b, kind, :, : part.shape[1]] += part

    def windowed(rows, count):
        return jnp.where(real_places(count), winf[rows, :], 0.0).astype(BF)

    def attention_forward(b, n, x, out, hook):
        lanes = head_of_lane()

        @pl.loop(0, CELLS // TILE)
        def _(t):
            rows = row_block(t, TILE)
            xhat, _ = standardized(x[rows, :].astype(F32))
            canvf[rows, :] = xhat * vector(b, 0) + vector(b, 1)

        to_windows(canvf, winf, SHIFT * b)
        to_windows(code.at[n], codew, SHIFT * b)

        @pl.loop(0, 4)
        def _(t):
            rows = row_block(t, 256)
            hq = windowed(rows, 256)
            hqw[n, rows, :] = hq
            for part in range(3):
                cols = slice(part * D, (part + 1) * D)
                acc = nn(hq, wat[b, :, cols]) + vec[b * 8 + 6 : b * 8 + 7, cols]
                if part == 0:
                    acc = acc * SCALE
                qkv[n, rows, cols] = acc.astype(BF)

        hook(0)

        @pl.loop(0, WINDOWS)
        def _(w):
            rows = row_block(w, PLACES)
            cells = codew[rows, :]
            region = (cells >> 1) * b
            pad = (cells & 1).astype(F32)
            lane = lax.broadcasted_iota(jnp.int32, (PLACES, 128), 1)
            same = jnp.where(lane == region, 1.0, 0.0)
            left = jnp.where(lane == 127, 1.0 - pad, same).astype(BF)
            right = jnp.where(lane == 127, -pad, same).astype(BF)
            agree = nt(left, jnp.concatenate([right, right], axis=0))
            mask = jnp.where(agree > 0.5, 0.0, MASKED)
            mask = jnp.concatenate([mask, mask], axis=1)
            for g in range(GROUPS):
                q = qkv[n, rows, g * 128 : (g + 1) * 128]
                k = qkv[n, rows, D + g * 128 : D + (g + 1) * 128]
                v = qkv[n, rows, 2 * D + g * 128 : 2 * D + (g + 1) * 128]
                s = nt(k, by_head(q, lanes)) + bias[b, g] + mask
                e = jnp.exp(s - jnp.max(s, axis=0, keepdims=True))
                p = (e * (1.0 / jnp.sum(e, axis=0, keepdims=True))).astype(BF)
                probs[n, w * GROUPS + g] = p
                att[n, rows, g * 128 : (g + 1) * 128] = own_head(tn(p, v), lanes).astype(BF)

        hook(1)

        @pl.loop(0, 4)
        def _(t):
            rows = row_block(t, 256)
            winf[rows, :] = nn(att[n, rows, :], wat[b, :, 3 * D :])

        to_canvas(winf, canvf, SHIFT * b)

        @pl.loop(0, CELLS // TILE)
        def _(t):
            rows = row_block(t, TILE)
            out[rows, :] = (x[rows, :].astype(F32) + (canvf[rows, :] + vector(b, 2))).astype(BF)

    def mlp_forward(b, n, x, out, hook):
        @pl.loop(0, CELLS // TILE)
        def _(t):
            rows = row_block(t, TILE)
            xhat, _ = standardized(x[rows, :].astype(F32))
            hq2[n, rows, :] = (xhat * vector(b, 3) + vector(b, 4)).astype(BF)

        @pl.loop(0, FF // 256)
        def _(i):
            cols = pl.ds(pl.multiple_of(i * 256, 256), 256)
            pre = nn(hq2[n], fc1[b, :, cols]) + vec[b * 8 + 7 : b * 8 + 8, cols]
            for at in range(0, CELLS, 16):
                h, dg = gelu_parts(pre[at : at + 16])
                hid[n, at : at + 16, cols] = h.astype(BF)
                dgelu[n, at : at + 16, cols] = dg.astype(BF)

        hook(0)
        total = nn(hid[n], fc2[b])
        for at in range(0, CELLS, TILE):
            rows = slice(at, at + TILE)
            out[rows, :] = (x[rows, :].astype(F32) + (total[rows] + vector(b, 5))).astype(BF)

    def norm_backward(b, kind, x, gz, out):
        @pl.loop(0, CELLS // TILE)
        def _(t):
            rows = row_block(t, TILE)
            xhat, rs = standardized(x[rows, :].astype(F32))
            gn = canvf[rows, :]
            gzf = gz[rows, :].astype(F32)
            add_vec(b, kind, by_eights(gn * xhat))
            add_vec(b, kind + 1, by_eights(gn))
            add_vec(b, 5 if kind else 2, by_eights(gzf))
            g = gn * vector(b, kind)
            mg = jnp.mean(g, axis=-1, keepdims=True)
            mgx = jnp.mean(g * xhat, axis=-1, keepdims=True)
            out[rows, :] = (gzf + rs * (g - mg - xhat * mgx)).astype(BF)

    def mlp_backward(b, n, x, gz, out, free_out, hook):
        wide_t[0, :, :CELLS] = hq2[n].T
        wide_t[1, :, :CELLS] = gz[...].T

        @pl.loop(0, FF // 256)
        def _(i):
            cols = pl.ds(pl.multiple_of(i * 256, 256), 256)
            gh = nt(gz[...], fc2[b, cols, :])
            sums = jnp.zeros((8, 256), F32)
            for at in range(0, CELLS, 16):
                gp = (gh[at : at + 16] * dgelu[n, at : at + 16, cols].astype(F32)).astype(BF)
                dgelu[n, at : at + 16, cols] = gp
                sums = sums + by_eights(gp.astype(F32))
            g_vec[b, 7, :, cols] += sums
            g_fc1[:, cols] += nn(wide_t[0, :, :CELLS], dgelu[n, :, cols])
            g_fc2t[:, cols] += nn(wide_t[1, :, :CELLS], hid[n, :, cols])

        hook(0)
        canvf[...] = nt(dgelu[n], fc1[b])
        free_out()
        norm_backward(b, 3, x, gz, out)

    def attention_backward(b, n, x, gz, out, free_out, hook):
        lanes = head_of_lane()

        @pl.loop(0, CELLS // TILE)
        def _(t):
            rows = row_block(t, TILE)
            canvf[rows, :] = gz[rows, :].astype(F32)

        to_windows(canvf, winf, SHIFT * b)

        @pl.loop(0, 4)
        def _(t):
            rows = row_block(t, 256)
            gzw[rows, :] = windowed(rows, 256)

        g_proj[...] += tn(att[n], gzw[...])

        @pl.loop(0, 4)
        def _(t):
            rows = row_block(t, 256)
            go[rows, :] = nt(gzw[rows, :], wat[b, :, 3 * D :]).astype(BF)

        hook(0)

        @pl.loop(0, WINDOWS)
        def _(w):
            rows = row_block(w, PLACES)
            for g in range(GROUPS):
                at = [slice(part * D + g * 128, part * D + (g + 1) * 128) for part in range(3)]
                q, k, v = (qkv[n, rows, cols] for cols in at)
                go_wide = by_head(go[rows, at[0]], lanes)
                p_low = probs[n, w * GROUPS + g]
                p = p_low.astype(F32)
                pd = p * nt(v, go_wide)
                ds = (pd - p * jnp.sum(pd, axis=0, keepdims=True)).astype(BF)
                g_tab[b, :, g * 256 : (g + 1) * 256] += ds.astype(F32)
                gqkv[rows, at[0]] = (own_head(tn(ds, k), lanes) * SCALE).astype(BF)
                gqkv[rows, at[1]] = nn(ds, by_head(q, lanes)).astype(BF)
                gqkv[rows, at[2]] = nn(p_low, go_wide).astype(BF)

        hook(1)

        @pl.loop(0, 4)
        def _(t):
            rows = row_block(t, 256)
            gq = gqkv[rows, :]
            add_vec(b, 6, by_eights(gq.astype(F32)))
            winf[rows, :] = nt(gq, wat[b, :, : 3 * D])

        to_canvas(winf, canvf, SHIFT * b)
        free_out()
        norm_backward(b, 0, x, gz, out)

    def attention_weights(n):
        wide_t[0] = hqw[n].T
        for part in range(3):
            cols = slice(part * D, (part + 1) * D)
            g_qkv[:, cols] += nn(wide_t[0], gqkv[:, cols])

    def partner(k):
        x, y = me % 2, me // 2
        return 2 * (1 - y if k & 2 else y) + (1 - x if k & 1 else x)

    def act_copies(n):
        away = [
            remote(
                buf.at[partner(k), n],
                r.act_hbm.at[me, n],
                r.act_send.at[k - 1, n],
                r.act_recv.at[k - 1, n],
                {"pipe": partner(k)},
            )
            for k in (2, 1, 3)
        ]
        return away, pltpu.make_async_copy(buf.at[me, n], r.act_hbm.at[me, n], r.local_sem.at[0, n])

    def send_acts(n):
        away, local = act_copies(n)
        for copy in away:
            copy.start()
        local.start()

    def acts_sent(n):
        away, local = act_copies(n)
        for copy in away:
            copy.wait_send()
        local.wait()

    def push(s, n, start):
        src = buf.at[s, n]
        dst = r.igrad_hbm.at[me, n]
        local = pltpu.make_async_copy(src, dst, r.local_sem.at[1, n])
        away = remote(src, dst, r.send_sem.at[s, n], r.recv_sem.at[me, n], {"pipe": s})

        @pl.when(me == s)
        def _():
            local.start() if start else local.wait()

        @pl.when(me != s)
        def _():
            away.start() if start else away.wait_send()

    def arrived(k, n):
        sender = partner(k)
        got = r.act_hbm.at[sender, n]
        remote(got, got, r.act_send.at[k - 1, n], r.act_recv.at[k - 1, n], {"pipe": sender}).wait_recv()
        got = r.igrad_hbm.at[sender, n]
        remote(got, got, r.send_sem.at[0, n], r.recv_sem.at[sender, n], {"pipe": sender}).wait_recv()

    attention_stash = ((hqw, r.h_hqw), (qkv, r.h_qkv), (probs, r.h_probs), (att, r.h_att))
    mlp_stash = ((hq2, r.h_hq2), (hid, r.h_hid), (dgelu, r.h_dgelu))

    def stash(sec, n, back):
        pairs = mlp_stash if sec else attention_stash
        return [
            pltpu.make_async_copy(*((far.at[n], near.at[n]) if back else (near.at[n], far.at[n])), r.st_sem.at[sec, n, i])
            for i, (near, far) in enumerate(pairs)
        ]

    def load(src, n):
        return pltpu.make_async_copy(src.at[me, n], inb.at[n], r.in_sem.at[n])

    def start(copies):
        for copy in copies:
            copy.start()

    def wait(copies):
        for copy in copies:
            copy.wait()

    steps = (step_1, step_2, step_3, step_4, step_5)
    schedule = {
        (2, 0, 0): ((2, 3),),
        (2, 1, 1): ((3, 3),),
        (1, 0, 0): ((2, 2),),
        (1, 1, 0): ((4, 3),),
        (0, 0, 0): ((3, 2), (2, 1), (5, 3)),
        (0, 0, 1): ((4, 2),),
        (0, 1, 0): ((5, 2),),
        (0, 1, 1): ((3, 1),),
    }
    after = {3: ((1, 3),), 2: ((1, 2),), 1: ((1, 1),), 0: ()}
    weight_steps = (weights_1, weights_2, weights_3, weights_4) if linked else ()
    gathering = {
        (0, 0): ((2, 1),),
        (0, 1): ((2, 2), (2, 3), (3, 1)),
        (0, 3): ((4, 1), (3, 2)),
        (1, 3): ((4, 2),),
        (2, 0): ((3, 3),),
        (2, 3): ((4, 3),),
    }

    codes = [pltpu.make_async_copy(r.code_hbm, code, r.code_sem.at[0])]
    start(codes)
    start([load(r.x_hbm, n) for n in range(canvases)])
    wait(codes)

    @pl.loop(0, canvases)
    def _(n):
        def gather(sec, i):
            todo = gathering.get((sec, i), ())
            if linked and todo:

                @pl.when(n == 0)
                def _():
                    for step, of in todo:
                        weight_steps[step - 1](of)

        load(r.x_hbm, n).wait()
        x = inb.at[n]
        for s in range(4):
            if s >= 2:
                wait(stash(s - 2, n, False))
            forward = mlp_forward if s % 2 else attention_forward
            forward(s // 2, n, x, buf.at[s, n], functools.partial(gather, s))
            x = buf.at[s, n]
            if s == 3:
                send_acts(n)
            if s < 2:
                start(stash(s, n, False))
            if s == 0:
                load(r.cot_hbm, n).start()
            gather(s, 3)

    for s in (3, 2, 1, 0):
        cleared(*((g_fc1, g_fc2t) if s % 2 else (g_qkv, g_proj)))

        @pl.loop(0, canvases)
        def _(n):
            def hook(i):
                for at in range(2):
                    todo = schedule.get((s, at, i), ())
                    if linked and todo:

                        @pl.when(n == (canvases - 1 if at else 0))
                        def _():
                            for step, of in todo:
                                steps[step - 1](of)

            if s == 3:
                load(r.cot_hbm, n).wait()
            if s == 0:
                load(r.x_hbm, n).wait()
            if s < 2:
                wait(stash(s, n, True))
            x = buf.at[s - 1, n] if s else inb.at[n]
            gz = inb.at[n] if s == 3 else buf.at[s + 1, n]
            backward = mlp_backward if s % 2 else attention_backward
            free_out = functools.partial(acts_sent, n) if s == 3 else lambda: None
            backward(s // 2, n, x, gz, buf.at[s, n], free_out, hook)
            if s % 2 == 0:
                attention_weights(n)
            if s == 2:
                push(3, n, True)
            if s:
                if s < 3:
                    push(s, n, True)
            else:

                @pl.when(n < canvases - 1)
                def _():
                    push(0, n, True)

            if s == 3:
                load(r.x_hbm, n).start()
            if s >= 2:
                start(stash(s - 2, n, True))

        if linked:
            for step, of in after[s]:
                steps[step - 1](of)
        else:
            whole = ((g_fc1, r.f_fc1), (g_fc2t, r.f_fc2t)) if s % 2 else ((g_qkv, r.f_qkv), (g_proj, r.f_proj))
            copies = [pltpu.make_async_copy(a, o.at[s // 2], r.go_sem.at[s, i]) for i, (a, o) in enumerate(whole)]
            start(copies)
            wait(copies)

    if linked:
        step_1(0)
        step_4(1)
        step_2(0)
    push(0, canvases - 1, True)
    if linked:
        step_5(1)
        smalls_sent(1)
        step_3(0)
        step_4(0)
        step_5(0)
        reductions_done()
        weights_sent()
        for k in range(1, 8):
            pack_copy(k).wait_send()
    for k in range(1, 4):
        for n in range(canvases):
            arrived(k, n)
    for s in range(4):
        for n in range(canvases):
            push(s, n, False)


def compute(linked, operands):
    canvases = operands["x_hbm"].shape[1]
    shape = jax.ShapeDtypeStruct
    hbm = pl.BlockSpec(memory_space=pl.ANY)
    vmem = pl.BlockSpec(memory_space=pltpu.VMEM)
    dma = pltpu.SemaphoreType.DMA
    full = {
        "wat": ((2, D, 4 * D), BF),
        "fc1": ((2, D, FF), BF),
        "fc2": ((2, FF, D), BF),
        "vec": ((16, FF), F32),
    }
    grads = {
        "g_qkv": ((D, 3 * D), F32),
        "g_proj": ((D, D), F32),
        "g_fc1": ((D, FF), F32),
        "g_fc2t": ((D, FF), F32),
        "g_vec": ((2, 8, 8, FF), F32),
        "g_tab": ((2, PLACES, GROUPS * 256), F32),
    }
    outs = {"act_hbm": ((4, canvases, CELLS, D), BF), "igrad_hbm": ((4, canvases, CELLS, D), BF)}
    kept = {
        "hqw": ((canvases, WROWS, D), BF),
        "qkv": ((canvases, WROWS, 3 * D), BF),
        "probs": ((canvases, WINDOWS * GROUPS, PLACES, 256), BF),
        "att": ((canvases, WROWS, D), BF),
        "hq2": ((canvases, CELLS, D), BF),
        "hid": ((canvases, CELLS, FF), BF),
        "dgelu": ((canvases, CELLS, FF), BF),
    }
    outs |= {"h_" + name: kind for name, kind in kept.items()}
    scratch = kept | {
        "inb": ((canvases, CELLS, D), BF),
        "code": ((canvases, CELLS, 128), jnp.int32),
        "codew": ((WROWS, 128), jnp.int32),
        "buf": ((4, canvases, CELLS, D), BF),
        "canvf": ((CELLS, D), F32),
        "winf": ((WROWS, D), F32),
        "gzw": ((WROWS, D), BF),
        "go": ((WROWS, D), BF),
        "gqkv": ((WROWS, 3 * D), BF),
        "wide_t": ((2, D, WROWS), BF),
    }
    sems = {
        "in_sem": (canvases,),
        "code_sem": (1,),
        "st_sem": (2, canvases, 4),
        "local_sem": (2, canvases),
        "act_send": (3, canvases),
        "act_recv": (3, canvases),
        "send_sem": (4, canvases),
        "recv_sem": (4, canvases),
    }
    if linked:
        outs |= {
            "o_qkv": ((2, 48, 3 * D), F32),
            "o_proj": ((2, 48, D), F32),
            "o_fc1": ((2, 48, FF), F32),
            "o_fc2": ((2, 192, D), F32),
            "o_small": ((2, 8, 64, D), BF),
        }
        scratch |= full | grads
        scratch |= {
            "packs": ((8, 16, 256), BF),
            "l_qkv": ((48, 3 * D), F32),
            "l_proj": ((48, D), F32),
            "l_fc1": ((48, FF), F32),
            "l_fc2": ((192, D), F32),
        }
        for kind, rows in (("m_", MLP_ROWS), ("a_", ATT_ROWS)):
            scratch |= {
                kind + "st_a": ((4, rows, D), BF),
                kind + "rc_a": ((4, rows, D), BF),
                kind + "st_b": ((3, rows, D), BF),
                kind + "rc_b": ((3, rows, D), BF),
                kind + "st_c": ((rows, D), BF),
                kind + "rc_c": ((3, rows // 4, D), BF),
                kind + "fin": ((rows, D), BF),
            }
        sems |= {
            "sh_sem": (4, 2),
            "os_sem": (2,),
            "go_sem": (4, 2),
            "wz_send": (4, 2, 3),
            "wz_recv": (4, 2, 3),
            "wx_send": (4, 2, 3, 3),
            "wx_recv": (4, 2, 3, 3),
            "ws_send": (4, 2, 4),
            "ws_recv": (4, 2, 4),
            "pk_send": (7,),
            "pk_recv": (7,),
            "ra_send": (4,),
            "ra_recv": (4,),
            "rb_send": (4, 3),
            "rb_recv": (4, 3),
            "rc_send": (4, 3),
            "rc_recv": (4, 3),
            "rf_send": (4, 3),
            "rf_recv": (4, 3),
            "rs_send": (2, 7),
            "rs_recv": (2, 7),
        }
    else:
        for name in ("g_vec", "g_tab"):
            outs[name] = grads.pop(name)
        outs |= {name.replace("g_", "f_"): ((2,) + dims, F32) for name, (dims, _) in grads.items()}
        scratch |= grads
        sems["go_sem"] = (4, 2)
    in_vmem = set(full) | {"bias", "pack", "g_vec", "g_tab"}
    names = tuple(operands) + tuple(outs) + tuple(scratch) + tuple(sems)
    results = pl.pallas_call(
        functools.partial(kernel, names, linked, canvases),
        out_shape=tuple(shape(*o) for o in outs.values()),
        in_specs=[vmem if name in in_vmem else hbm for name in operands],
        out_specs=tuple(vmem if name in in_vmem else hbm for name in outs),
        scratch_shapes=[pltpu.VMEM(*v) for v in scratch.values()] + [dma(v) for v in sems.values()],
        compiler_params=pltpu.CompilerParams(
            vmem_limit_bytes=64 * 1024 * 1024 - 65536, collective_id=0, has_side_effects=True
        ),
    )(*operands.values())
    return dict(zip(outs, results))


def place_pairs():
    place = np.arange(PLACES)
    r, c = place // 8, place % 8
    index = (r[None, :] - r[:, None] + WIN - 1) * (2 * WIN - 1) + c[None, :] - c[:, None] + WIN - 1
    real = (r < WIN) & (c < WIN)
    return index, real[:, None] & real[None, :], real


def pair_onehot():
    index, both, _ = place_pairs()
    table = (2 * WIN - 1) ** 2
    hot = (np.where(both, index, -1).reshape(-1)[None, :] == np.arange(table)[:, None])
    return hot.astype(np.float32)


def body(
    inputs,
    cotangent,
    pad_mask,
    region_ids,
    norm1_gain,
    norm1_bias,
    qkv_weight,
    qv_bias,
    rel_table,
    proj_weight,
    proj_bias,
    norm2_gain,
    norm2_bias,
    fc1_weight,
    fc1_bias,
    fc2_weight,
    fc2_bias,
):
    owners = lax.axis_size("dp")
    linked = owners == 8
    mine = lax.axis_index("pipe")

    def own(a):
        return lax.dynamic_index_in_dim(a, mine, 0, keepdims=False)

    code = own(region_ids) * 2 + own(pad_mask)
    code = jnp.broadcast_to(code[:, :, None], code.shape + (128,))

    hot = pair_onehot()
    _, _, real = place_pairs()
    rel = lax.dot_general(
        rel_table.astype(BF), jnp.asarray(hot, BF), (((1,), (0,)), ((), ())), preferred_element_type=F32
    )
    rel = rel.reshape(2, GROUPS, 4, PLACES, PLACES).transpose(0, 1, 3, 2, 4)
    rel = jnp.where(jnp.asarray(real)[None, None, :, None, None], rel, MASKED)
    rel = rel.reshape(2, GROUPS, PLACES, 256)

    operands = {"x_hbm": inputs, "cot_hbm": cotangent, "code_hbm": code, "bias": rel}
    vectors = (norm1_gain, norm1_bias, proj_bias, norm2_gain, norm2_bias, fc2_bias, qv_bias, fc1_bias)
    sizes = [v.shape[1] for v in vectors]
    ends = np.cumsum([0] + sizes)
    if linked:
        pack = jnp.stack([jnp.pad(v, ((0, 0), (0, 256 - v.shape[1]))) for v in vectors], axis=1)
        operands |= {
            "pack": pack.reshape(16, 256).astype(BF),
            "s_qkv": qkv_weight,
            "s_proj": proj_weight,
            "s_fc1": fc1_weight,
            "s_fc2": fc2_weight,
        }
    else:

        def gathered(a):
            return lax.all_gather(a.astype(BF), "dp", axis=1, tiled=True)

        packed = lax.all_gather(jnp.concatenate(vectors, axis=1).astype(BF), "dp", axis=1)
        parts = [packed[:, :, a:b].reshape(2, -1).astype(F32) for a, b in zip(ends[:-1], ends[1:])]
        qv = parts[6]
        parts[6] = jnp.concatenate([qv[:, :D], jnp.zeros_like(qv[:, :D]), qv[:, D:]], axis=1)
        vec = jnp.stack([jnp.pad(p, ((0, 0), (0, FF - p.shape[1]))) for p in parts], axis=1)
        operands |= {
            "wat": jnp.concatenate([gathered(qkv_weight), gathered(proj_weight)], axis=2),
            "fc1": gathered(fc1_weight),
            "fc2": gathered(fc2_weight),
            "vec": vec.reshape(16, FF),
        }

    out = compute(linked, operands)

    def to_owners(g):
        shared = lax.psum_scatter(g, "dp", scatter_dimension=1, tiled=True)
        return lax.psum(shared, "pipe")

    if linked:
        small = out["o_small"]
        g_tab = jnp.concatenate([small[:, :, :8], small[:, :, 8:16]], axis=3).reshape(2, PLACES, GROUPS * 256)
        g_vec = jnp.concatenate([small[:, :, 16 + 8 * j : 24 + 8 * j] for j in range(4)], axis=3)
    else:
        g_tab, g_vec = out["g_tab"], out["g_vec"]

    g_vec = jnp.sum(g_vec.astype(F32), axis=2)
    kinds = [g_vec[:, i] for i in range(8)]
    qv_sum = jnp.concatenate([kinds[6][:, :D], kinds[6][:, 2 * D : 3 * D]], axis=1)
    rows = [kinds[0], kinds[1], kinds[2], kinds[3], kinds[4], kinds[5], qv_sum, kinds[7]]
    if linked:
        at = lax.axis_index("dp")
        small = [lax.dynamic_slice_in_dim(v, at * n, n, 1) for v, n in zip(rows, sizes)]
    else:
        rows = [v[:, : n * owners].reshape(2, -1, n) for v, n in zip(rows, sizes)]
        g_small = to_owners(jnp.concatenate(rows, axis=2))[:, 0]
        small = [g_small[:, a:b] for a, b in zip(ends[:-1], ends[1:])]

    pairs = g_tab.reshape(2, PLACES, HEADS, PLACES).transpose(0, 2, 1, 3)
    pairs = pairs.reshape(2, HEADS, PLACES * PLACES)
    g_table = lax.dot_general(
        jnp.broadcast_to(jnp.asarray(hot, pairs.dtype), (2,) + hot.shape),
        pairs,
        (((2,), (2,)), ((0,), (0,))),
        precision=None if linked else lax.Precision.HIGHEST,
        preferred_element_type=F32,
    )
    if linked:
        big = [out[name] for name in ("o_qkv", "o_proj", "o_fc1", "o_fc2")]
    else:
        g_table = lax.psum(g_table, ("pipe", "dp"))
        big = [to_owners(out[name]) for name in ("f_qkv", "f_proj", "f_fc1")]
        big.append(to_owners(out["f_fc2t"].transpose(0, 2, 1)))

    return (
        out["act_hbm"][None],
        out["igrad_hbm"][None],
        small[0],
        small[1],
        big[0],
        small[6],
        g_table,
        big[1],
        small[2],
        small[3],
        small[4],
        big[2],
        small[7],
        big[3],
        small[5],
    )


def solution(mesh):
    cols = P(None, "dp")
    rows = P(None, "dp", None)
    return jax.shard_map(
        body,
        mesh=mesh,
        in_specs=(
            P(None, "dp", None, None),
            P(None, "dp", None, None),
            rows,
            rows,
            cols,
            cols,
            rows,
            cols,
            P(),
            rows,
            cols,
            cols,
            cols,
            rows,
            cols,
            rows,
            cols,
        ),
        out_specs=(
            P("pipe", None, "dp", None, None),
            P("pipe", None, "dp", None, None),
            cols,
            cols,
            rows,
            cols,
            P(),
            rows,
            cols,
            cols,
            cols,
            rows,
            cols,
            rows,
            cols,
        ),
        check_vma=False,
    )
```

profile of v0, /device:TPU:0, one launch (start us, length us, event | category | flops | bytes accessed | tf_op | source)
XLA Modules:
  0.0 356.9 jit_solution(13415940564981880734)
XLA Ops:
  0.6 0.0 copy-start.5
  0.7 0.7 add_bitcast_fusion
  1.4 1.2 broadcast_in_dim.28.refs_2_
  2.5 0.7 convert_element_type.20
  3.3 1.7 convolution_bitcast_fusion
  5.0 0.3 copy.48
  5.4 0.5 reshape.62
  5.9 0.2 select_bitcast_fusion
  6.1 0.5 copy.49
  6.6 1.2 reshape.63.refs_3_
  8.1 0.6 copy.64
  8.7 330.5 %shard_map.307 = (bf16[4,2,784,384]{3,2,1,0:T(8,128)(2,1)}, bf16[4,2,784,384]{3,2,1,0:T(8,128)(2,1)}, bf16[2,1024,384]{2,1,0:T(8,128)(2,1)}, bf16[2,1024,1152]{2...) custom-call(bf16[4,2,784,384]{3,2,1,0:T(8,128)(2,1)} %refs_0_.1, ...), custom_call_target="tpu_custom_call" | custom-call | tf_op jit(solution)/shard_map/pallas_call | solution.py:990
  339.2 1.3 fusion.4
  340.5 0.3 convert_reduce_fusion
  340.8 0.1 fusion.5
  340.8 0.6 constant_dynamic-slice_fusion
  341.5 0.6 constant_dynamic-slice_fusion.3
  342.1 0.6 fusion.3
  342.8 0.6 constant_dynamic-slice_fusion.5
  343.4 0.1 constant_dynamic-slice_fusion.1
  343.5 0.6 copy.65
  344.1 0.3 reshape_reshape.3
  344.4 0.1 copy.54
  344.6 0.3 reshape.66
  344.9 0.8 fusion
  345.7 0.7 copy.53
  346.4 5.2 %copy.79 = bf16[1,4,2,784,384]{4,3,2,1,0:T(8,128)(2,1)} copy(bf16[1,4,2,784,384]{4,3,2,1,0:T(8,128)(2,1)} %bitcast.52) | data formatting | bytes 9633792
  351.7 2.2 copy.80
  353.9 0.8 copy.81
  354.6 0.7 copy.82
  355.3 0.8 copy.83
  356.1 0.8 copy.84
  (51 shorter events, 0.2 us)
Async XLA Ops:
  0.6 5.3 %copy-start.5 = (pred[64]{0:T(512)(128)(4,1)S(1)}, pred[64]{0:T(512)(128)(4,1)}, u32[]{:S(2)}) copy-start(pred[64]{0:T(512)(128)(4,1)} %constant.48.clone) | copy-start | bytes 196
  5.3 2.5 copy-start.6
  5.3 2.5 copy-start.7
  5.3 2.5 copy-start.8
  5.4 2.5 copy-start.9
  5.4 2.6 copy-start.10
  5.4 2.6 copy-start.11
  5.4 2.6 copy-start.12
  5.4 2.6 copy-start.4
  339.2 5.7 %copy-start.13 = (bf16[169,4096]{1,0:T(8,128)(2,1)S(1)}, bf16[169,4096]{1,0:T(8,128)(2,1)}, u32[]{:S(2)}) copy-start(bf16[169,4096]{1,0:T(8,128)(2,1)} %constant.47.clone) | copy-start | bytes 4153348
  346.4 5.2 %slice-start = ((s8[4816896]{0:T(1024)(128)(4,1)}), s8[4194304]{0:T(1024)(128)(4,1)S(1)}, s32[]{:S(2)}) async-start(s8[4816896]{0:T(1024)(128)(4,1)} %bitcast.49), calls=%async_computation | async-start | bytes 8388608
  346.4 5.2 %slice-start.1 = ((s8[4816896]{0:T(1024)(128)(4,1)}), s8[622592]{0:T(1024)(128)(4,1)S(1)}, s32[]{:S(2)}) async-start(s8[4816896]{0:T(1024)(128)(4,1)} %bitcast.49), calls=%async_computation.1 | async-start | bytes 1245184
  351.6 2.3 copy-start.2
  351.6 3.0 copy-start.3
  351.6 3.7 %copy-start.1 = (f32[2,48,1536]{2,1,0:T(8,128)S(1)}, f32[2,48,1536]{2,1,0:T(8,128)}, u32[]{:S(2)}) copy-start(f32[2,48,1536]{2,1,0:T(8,128)} %get-tuple-element.122) | copy-start | bytes 1769476
  351.6 4.5 %copy-start = (f32[2,192,384]{2,1,0:T(8,128)S(1)}, f32[2,192,384]{2,1,0:T(8,128)}, u32[]{:S(2)}) copy-start(f32[2,192,384]{2,1,0:T(8,128)} %get-tuple-element.124) | copy-start | bytes 1769476
where the time goes:
time: 358 us; the launch traced here: 357 us
  Pallas kernels  330 us (92%)
  local copies, waits for them, and re-layouts  20.3 us (6%)
    pallas_call x1, Pallas kernels, compute(): pl.pallas_call(functools.partial(kernel, names, linked, canvases), out_sh...  330 us
    unnamed x48, local copies, waits for them, and re-layouts  11.9 us

commit v1 on v0

--- a/solution.py
+++ b/solution.py
@@ -29,8 +29,7 @@
 BF = jnp.bfloat16
 F32 = jnp.float32
 
-ERF_P = 0.3275911 / np.sqrt(2.0)
-ERF_A = [0.5 * a for a in (0.254829592, -0.284496736, 1.421413741, -1.453152027, 1.061405429)]
+RSQRT_2 = 1.0 / np.sqrt(2.0)
 PHI_0 = 1.0 / np.sqrt(2.0 * np.pi)
 
 
@@ -87,16 +86,8 @@
 
 
 def gelu_parts(x):
-    den = 1.0 + ERF_P * jnp.abs(x)
-    t = pl.reciprocal(den, approx=True)
-    t = t * (2.0 - den * t)
-    e = jnp.exp(-0.5 * x * x)
-    poly = ERF_A[4]
-    for a in ERF_A[3::-1]:
-        poly = poly * t + a
-    tail = poly * t * e
-    cdf = jnp.where(x >= 0.0, 1.0 - tail, tail)
-    return x * cdf, cdf + x * (e * PHI_0)
+    cdf = 0.5 + 0.5 * lax.erf(x * RSQRT_2)
+    return x * cdf, cdf + x * (jnp.exp(-0.5 * x * x) * PHI_0)
 
 
 def real_places(rows):
@@ -108,16 +99,22 @@
     return lax.broadcasted_iota(jnp.int32, (PLACES, 128), 1) >> 5
 
 
-def by_head(x, lanes):
+def by_low(x, lanes):
     zero = jnp.zeros_like(x)
-    return jnp.concatenate([jnp.where(lanes == h, x, zero) for h in range(4)], axis=0)
-
-
-def own_head(wide, lanes):
-    out = wide[3 * PLACES :]
-    for h in (2, 1, 0):
-        out = jnp.where(lanes == h, wide[h * PLACES : (h + 1) * PLACES], out)
-    return out
+    return jnp.concatenate([jnp.where((lanes & 1) == h, x, zero) for h in range(2)], axis=0)
+
+
+def by_high(x, lanes):
+    zero = jnp.zeros_like(x)
+    return jnp.concatenate([jnp.where((lanes >> 1) == h, x, zero) for h in range(2)], axis=0)
+
+
+def own_low(wide, lanes):
+    return jnp.where((lanes & 1) == 0, wide[:PLACES], wide[PLACES:])
+
+
+def own_high(wide, lanes):
+    return jnp.where((lanes >> 1) == 0, wide[:PLACES], wide[PLACES:])
 
 
 MESH = pl.DeviceIdType.MESH
@@ -132,8 +129,8 @@
     inb, code, codew, buf = r.inb, r.code, r.codew, r.buf
     hqw, qkv, probs, att = r.hqw, r.qkv, r.probs, r.att
     hq2, hid, dgelu = r.hq2, r.hid, r.dgelu
-    canvf, winf, gzw, wide_t, gqkv, go = r.canvf, r.winf, r.gzw, r.wide_t, r.gqkv, r.go
-    g_qkv, g_proj, g_fc1, g_fc2t, g_vec, g_tab = r.g_qkv, r.g_proj, r.g_fc1, r.g_fc2t, r.g_vec, r.g_tab
+    canvf, winf, gzw, gqkv, go = r.canvf, r.winf, r.gzw, r.gqkv, r.go
+    g_qkv, g_proj, g_fc1, g_fc2, g_vec, g_tab = r.g_qkv, r.g_proj, r.g_fc1, r.g_fc2, r.g_vec, r.g_tab
     wat, fc1, fc2, vec, bias = r.wat, r.fc1, r.fc2, r.vec, r.bias
     if linked:
         d = lax.axis_index("dp")
@@ -266,13 +263,13 @@
                     out.append((len(out) * 48, 48, load))
 
         def small():
-            rows = pl.ds(pl.multiple_of(owner * 8, 8), 8)
-            parts = [g_tab[b, rows, j * D : (j + 1) * D] for j in range(2)]
+            parts = [g_tab[b, pl.ds(pl.multiple_of(owner * 16, 16), 16), :]]
             parts += [g_vec[b, owner, :, j * D : (j + 1) * D] for j in range(4)]
             return jnp.concatenate(parts + [jnp.zeros((16, D), F32)], axis=0)
 
         if sec % 2:
             matrix(g_fc1, 48)
+            matrix(g_fc2, 192)
         else:
             matrix(g_qkv, 48)
             matrix(g_proj, 48)
@@ -299,12 +296,6 @@
                 q.st_a[i, row : row + rows, :] = load().astype(BF)
             for row, rows, load in pieces(sec, 2 * i + c):
                 kept[row : row + rows, :] = load().astype(BF)
-            if sec % 2:
-                winf[:D, :] = g_fc2t[:, pl.ds(pl.multiple_of(i * D, 128), D)].T
-                for t in range(0, 192, 48):
-                    at = slice(192 + t, 240 + t)
-                    q.st_a[i, at, :] = winf[pl.ds(pl.multiple_of((1 - c) * 192 + t, 16), 48), :].astype(BF)
-                    kept[at, :] = winf[pl.ds(pl.multiple_of(c * 192 + t, 16), 48), :].astype(BF)
         copy_a(sec).start()
 
     def copy_a(sec):
@@ -439,7 +430,7 @@
                 ).wait_recv()
 
     if linked:
-        lands = ((r.s_qkv, g_qkv, wat, 0), (r.s_proj, g_proj, wat, 3 * D), (r.s_fc1, g_fc1, fc1, 0), (r.s_fc2, g_fc2t, fc2, 0))
+        lands = ((r.s_qkv, g_qkv, wat, 0), (r.s_proj, g_proj, wat, 3 * D), (r.s_fc1, g_fc1, fc1, 0), (r.s_fc2, g_fc2, fc2, 0))
 
         def landing(i, b):
             src, dst, _, _ = lands[i]
@@ -483,8 +474,6 @@
         for k in range(1, 8):
             pack_arrival(k).wait_recv()
         place_vectors()
-        weights_3(0)
-        weights_4(0)
 
     def vector(b, kind, width=D):
         return vec[b * 8 + kind : b * 8 + kind + 1, :width]
@@ -506,6 +495,7 @@
 
         to_windows(canvf, winf, SHIFT * b)
         to_windows(code.at[n], codew, SHIFT * b)
+        hook(4)
 
         @pl.loop(0, 4)
         def _(t):
@@ -533,16 +523,19 @@
             right = jnp.where(lane == 127, -pad, same).astype(BF)
             agree = nt(left, jnp.concatenate([right, right], axis=0))
             mask = jnp.where(agree > 0.5, 0.0, MASKED)
-            mask = jnp.concatenate([mask, mask], axis=1)
             for g in range(GROUPS):
                 q = qkv[n, rows, g * 128 : (g + 1) * 128]
                 k = qkv[n, rows, D + g * 128 : D + (g + 1) * 128]
                 v = qkv[n, rows, 2 * D + g * 128 : 2 * D + (g + 1) * 128]
-                s = nt(k, by_head(q, lanes)) + bias[b, g] + mask
-                e = jnp.exp(s - jnp.max(s, axis=0, keepdims=True))
-                p = (e * (1.0 / jnp.sum(e, axis=0, keepdims=True))).astype(BF)
+                scores = nt(by_low(k, lanes), by_high(q, lanes)) + bias[b, g]
+                halves = []
+                for h in range(2):
+                    s = scores[h * PLACES : (h + 1) * PLACES] + mask
+                    e = jnp.exp(s - jnp.max(s, axis=0, keepdims=True))
+                    halves.append((e * (1.0 / jnp.sum(e, axis=0, keepdims=True))).astype(BF))
+                p = jnp.concatenate(halves, axis=0)
                 probs[n, w * GROUPS + g] = p
-                att[n, rows, g * 128 : (g + 1) * 128] = own_head(tn(p, v), lanes).astype(BF)
+                att[n, rows, g * 128 : (g + 1) * 128] = own_high(tn(p, by_low(v, lanes)), lanes).astype(BF)
 
         hook(1)
 
@@ -596,9 +589,6 @@
             out[rows, :] = (gzf + rs * (g - mg - xhat * mgx)).astype(BF)
 
     def mlp_backward(b, n, x, gz, out, free_out, hook):
-        wide_t[0, :, :CELLS] = hq2[n].T
-        wide_t[1, :, :CELLS] = gz[...].T
-
         @pl.loop(0, FF // 256)
         def _(i):
             cols = pl.ds(pl.multiple_of(i * 256, 256), 256)
@@ -609,8 +599,8 @@
                 dgelu[n, at : at + 16, cols] = gp
                 sums = sums + by_eights(gp.astype(F32))
             g_vec[b, 7, :, cols] += sums
-            g_fc1[:, cols] += nn(wide_t[0, :, :CELLS], dgelu[n, :, cols])
-            g_fc2t[:, cols] += nn(wide_t[1, :, :CELLS], hid[n, :, cols])
+            g_fc1[:, cols] += tn(hq2[n], dgelu[n, :, cols])
+            g_fc2[cols, :] += tn(hid[n, :, cols], gz[...])
 
         hook(0)
         canvf[...] = nt(dgelu[n], fc1[b])
@@ -647,15 +637,19 @@
             for g in range(GROUPS):
                 at = [slice(part * D + g * 128, part * D + (g + 1) * 128) for part in range(3)]
                 q, k, v = (qkv[n, rows, cols] for cols in at)
-                go_wide = by_head(go[rows, at[0]], lanes)
+                go_wide = by_high(go[rows, at[0]], lanes)
                 p_low = probs[n, w * GROUPS + g]
                 p = p_low.astype(F32)
-                pd = p * nt(v, go_wide)
-                ds = (pd - p * jnp.sum(pd, axis=0, keepdims=True)).astype(BF)
-                g_tab[b, :, g * 256 : (g + 1) * 256] += ds.astype(F32)
-                gqkv[rows, at[0]] = (own_head(tn(ds, k), lanes) * SCALE).astype(BF)
-                gqkv[rows, at[1]] = nn(ds, by_head(q, lanes)).astype(BF)
-                gqkv[rows, at[2]] = nn(p_low, go_wide).astype(BF)
+                pd = p * nt(by_low(v, lanes), go_wide)
+                halves = []
+                for h in range(2):
+                    half = slice(h * PLACES, (h + 1) * PLACES)
+                    halves.append((pd[half] - p[half] * jnp.sum(pd[half], axis=0, keepdims=True)).astype(BF))
+                ds = jnp.concatenate(halves, axis=0)
+                g_tab[b, :, g * 128 : (g + 1) * 128] += ds.astype(F32)
+                gqkv[rows, at[0]] = (own_high(tn(ds, by_low(k, lanes)), lanes) * SCALE).astype(BF)
+                gqkv[rows, at[1]] = own_low(nn(ds, by_high(q, lanes)), lanes).astype(BF)
+                gqkv[rows, at[2]] = own_low(nn(p_low, go_wide), lanes).astype(BF)
 
         hook(1)
 
@@ -671,10 +665,9 @@
         norm_backward(b, 0, x, gz, out)
 
     def attention_weights(n):
-        wide_t[0] = hqw[n].T
         for part in range(3):
             cols = slice(part * D, (part + 1) * D)
-            g_qkv[:, cols] += nn(wide_t[0], gqkv[:, cols])
+            g_qkv[:, cols] += tn(hqw[n], gqkv[:, cols])
 
     def partner(k):
         x, y = me % 2, me // 2
@@ -761,6 +754,7 @@
     after = {3: ((1, 3),), 2: ((1, 2),), 1: ((1, 1),), 0: ()}
     weight_steps = (weights_1, weights_2, weights_3, weights_4) if linked else ()
     gathering = {
+        (0, 4): ((3, 0), (4, 0)),
         (0, 0): ((2, 1),),
         (0, 1): ((2, 2), (2, 3), (3, 1)),
         (0, 3): ((4, 1), (3, 2)),
@@ -802,7 +796,7 @@
             gather(s, 3)
 
     for s in (3, 2, 1, 0):
-        cleared(*((g_fc1, g_fc2t) if s % 2 else (g_qkv, g_proj)))
+        cleared(*((g_fc1, g_fc2) if s % 2 else (g_qkv, g_proj)))
 
         @pl.loop(0, canvases)
         def _(n):
@@ -831,13 +825,12 @@
                 attention_weights(n)
             if s == 2:
                 push(3, n, True)
-            if s:
-                if s < 3:
-                    push(s, n, True)
-            else:
+                push(2, n, True)
+            if s == 0:
 
                 @pl.when(n < canvases - 1)
                 def _():
+                    push(1, n, True)
                     push(0, n, True)
 
             if s == 3:
@@ -849,7 +842,7 @@
             for step, of in after[s]:
                 steps[step - 1](of)
         else:
-            whole = ((g_fc1, r.f_fc1), (g_fc2t, r.f_fc2t)) if s % 2 else ((g_qkv, r.f_qkv), (g_proj, r.f_proj))
+            whole = ((g_fc1, r.f_fc1), (g_fc2, r.f_fc2)) if s % 2 else ((g_qkv, r.f_qkv), (g_proj, r.f_proj))
             copies = [pltpu.make_async_copy(a, o.at[s // 2], r.go_sem.at[s, i]) for i, (a, o) in enumerate(whole)]
             start(copies)
             wait(copies)
@@ -858,6 +851,7 @@
         step_1(0)
         step_4(1)
         step_2(0)
+    push(1, canvases - 1, True)
     push(0, canvases - 1, True)
     if linked:
         step_5(1)
@@ -893,15 +887,15 @@
         "g_qkv": ((D, 3 * D), F32),
         "g_proj": ((D, D), F32),
         "g_fc1": ((D, FF), F32),
-        "g_fc2t": ((D, FF), F32),
+        "g_fc2": ((FF, D), F32),
         "g_vec": ((2, 8, 8, FF), F32),
-        "g_tab": ((2, PLACES, GROUPS * 256), F32),
+        "g_tab": ((2, 2 * PLACES, GROUPS * 128), F32),
     }
     outs = {"act_hbm": ((4, canvases, CELLS, D), BF), "igrad_hbm": ((4, canvases, CELLS, D), BF)}
     kept = {
         "hqw": ((canvases, WROWS, D), BF),
         "qkv": ((canvases, WROWS, 3 * D), BF),
-        "probs": ((canvases, WINDOWS * GROUPS, PLACES, 256), BF),
+        "probs": ((canvases, WINDOWS * GROUPS, 128, 128), BF),
         "att": ((canvases, WROWS, D), BF),
         "hq2": ((canvases, CELLS, D), BF),
         "hid": ((canvases, CELLS, FF), BF),
@@ -918,7 +912,6 @@
         "gzw": ((WROWS, D), BF),
         "go": ((WROWS, D), BF),
         "gqkv": ((WROWS, 3 * D), BF),
-        "wide_t": ((2, D, WROWS), BF),
     }
     sems = {
         "in_sem": (canvases,),
@@ -1049,9 +1042,9 @@
     rel = lax.dot_general(
         rel_table.astype(BF), jnp.asarray(hot, BF), (((1,), (0,)), ((), ())), preferred_element_type=F32
     )
-    rel = rel.reshape(2, GROUPS, 4, PLACES, PLACES).transpose(0, 1, 3, 2, 4)
-    rel = jnp.where(jnp.asarray(real)[None, None, :, None, None], rel, MASKED)
-    rel = rel.reshape(2, GROUPS, PLACES, 256)
+    rel = rel.reshape(2, GROUPS, 2, 2, PLACES, PLACES)
+    rel = jnp.where(jnp.asarray(real)[None, None, None, None, :, None], rel, MASKED)
+    rel = rel.transpose(0, 1, 3, 4, 2, 5).reshape(2, GROUPS, 128, 128)
 
     operands = {"x_hbm": inputs, "cot_hbm": cotangent, "code_hbm": code, "bias": rel}
     vectors = (norm1_gain, norm1_bias, proj_bias, norm2_gain, norm2_bias, fc2_bias, qv_bias, fc1_bias)
@@ -1091,7 +1084,7 @@
 
     if linked:
         small = out["o_small"]
-        g_tab = jnp.concatenate([small[:, :, :8], small[:, :, 8:16]], axis=3).reshape(2, PLACES, GROUPS * 256)
+        g_tab = small[:, :, :16].reshape(2, 128, GROUPS * 128)
         g_vec = jnp.concatenate([small[:, :, 16 + 8 * j : 24 + 8 * j] for j in range(4)], axis=3)
     else:
         g_tab, g_vec = out["g_tab"], out["g_vec"]
@@ -1108,7 +1101,7 @@
         g_small = to_owners(jnp.concatenate(rows, axis=2))[:, 0]
         small = [g_small[:, a:b] for a, b in zip(ends[:-1], ends[1:])]
 
-    pairs = g_tab.reshape(2, PLACES, HEADS, PLACES).transpose(0, 2, 1, 3)
+    pairs = g_tab.reshape(2, 2, PLACES, GROUPS, 2, PLACES).transpose(0, 3, 4, 1, 2, 5)
     pairs = pairs.reshape(2, HEADS, PLACES * PLACES)
     g_table = lax.dot_general(
         jnp.broadcast_to(jnp.asarray(hot, pairs.dtype), (2,) + hot.shape),
@@ -1121,8 +1114,7 @@
         big = [out[name] for name in ("o_qkv", "o_proj", "o_fc1", "o_fc2")]
     else:
         g_table = lax.psum(g_table, ("pipe", "dp"))
-        big = [to_owners(out[name]) for name in ("f_qkv", "f_proj", "f_fc1")]
-        big.append(to_owners(out["f_fc2t"].transpose(0, 2, 1)))
+        big = [to_owners(out[name]) for name in ("f_qkv", "f_proj", "f_fc1", "f_fc2")]
 
     return (
         out["act_hbm"][None],

time: 358 us -> 352 us (0.983)
  Pallas kernels: 330 us -> 324 us
    pallas_call x1, Pallas kernels: 330 us -> 324 us  [compute(): pl.pallas_call(functools.partial(kernel, names, linked, canvases), out_sh...]
where the time goes in v1:
time: 352 us
  Pallas kernels  324 us (92%)
  local copies, waits for them, and re-layouts  21.1 us (6%)
    pallas_call x1, Pallas kernels, compute(): pl.pallas_call(functools.partial(kernel, names, linked, canvases), out_sh...  324 us
    unnamed x48, local copies, waits for them, and re-layouts  11.9 us

profile of v1, /device:TPU:0, one launch (start us, length us, event | category | flops | bytes accessed | tf_op | source)
XLA Modules:
  0.0 351.7 jit_solution(7400624179946267944)
XLA Ops:
  0.7 0.7 add_bitcast_fusion
  1.4 1.2 broadcast_in_dim.28.refs_2_
  2.5 0.7 convert_element_type.20
  3.3 1.7 convolution_bitcast_fusion
  5.0 0.3 copy.48
  5.4 0.5 reshape.62
  5.9 0.2 select_bitcast_fusion
  6.1 0.6 copy.49
  6.7 1.2 reshape.63.refs_3_
  8.2 0.6 copy.66
  8.8 324.5 %shard_map.307 = (bf16[4,2,784,384]{3,2,1,0:T(8,128)(2,1)}, bf16[4,2,784,384]{3,2,1,0:T(8,128)(2,1)}, bf16[2,1024,384]{2,1,0:T(8,128)(2,1)}, bf16[2,1024,1152]{2...) custom-call(bf16[4,2,784,384]{3,2,1,0:T(8,128)(2,1)} %refs_0_.1, ...), custom_call_target="tpu_custom_call" | custom-call | tf_op jit(solution)/shard_map/pallas_call | solution.py:983
  333.3 1.2 fusion.5
  334.5 0.3 convert_reduce_fusion
  334.7 0.1 fusion.6
  334.8 0.6 constant_dynamic-slice_fusion
  335.5 0.6 constant_dynamic-slice_fusion.3
  336.1 0.6 fusion.4
  336.8 0.6 constant_dynamic-slice_fusion.5
  337.4 0.1 constant_dynamic-slice_fusion.1
  337.5 0.6 copy.67
  338.1 0.9 slice.54
  339.0 0.2 reshape_reshape.3
  339.2 0.1 copy.64
  339.3 0.3 reshape.64
  339.6 0.8 fusion
  340.5 0.7 copy.53
  341.1 5.2 %copy.81 = bf16[1,4,2,784,384]{4,3,2,1,0:T(8,128)(2,1)} copy(bf16[1,4,2,784,384]{4,3,2,1,0:T(8,128)(2,1)} %bitcast.55) | data formatting | bytes 9633792
  346.4 2.2 copy.82
  348.6 0.8 copy.83
  349.4 0.7 copy.84
  350.0 0.8 copy.85
  350.9 0.8 copy.86
  (51 shorter events, 0.2 us)
Async XLA Ops:
  0.6 5.3 %copy-start.5 = (pred[64]{0:T(512)(128)(4,1)S(1)}, pred[64]{0:T(512)(128)(4,1)}, u32[]{:S(2)}) copy-start(pred[64]{0:T(512)(128)(4,1)} %constant.48.clone) | copy-start | bytes 196
  5.3 2.6 copy-start.6
  5.3 2.6 copy-start.7
  5.3 2.6 copy-start.8
  5.4 2.6 copy-start.9
  5.4 2.7 copy-start.10
  5.4 2.7 copy-start.11
  5.4 2.7 copy-start.12
  5.4 2.7 copy-start.4
  333.3 6.4 %copy-start.13 = (bf16[169,4096]{1,0:T(8,128)(2,1)S(1)}, bf16[169,4096]{1,0:T(8,128)(2,1)}, u32[]{:S(2)}) copy-start(bf16[169,4096]{1,0:T(8,128)(2,1)} %constant.47.clone) | copy-start | bytes 4153348
  341.1 5.2 %slice-start = ((s8[4816896]{0:T(1024)(128)(4,1)}), s8[4194304]{0:T(1024)(128)(4,1)S(1)}, s32[]{:S(2)}) async-start(s8[4816896]{0:T(1024)(128)(4,1)} %bitcast.52), calls=%async_computation | async-start | bytes 8388608
  341.1 5.2 %slice-start.1 = ((s8[4816896]{0:T(1024)(128)(4,1)}), s8[622592]{0:T(1024)(128)(4,1)S(1)}, s32[]{:S(2)}) async-start(s8[4816896]{0:T(1024)(128)(4,1)} %bitcast.52), calls=%async_computation.1 | async-start | bytes 1245184
  346.4 2.3 copy-start.2
  346.4 3.0 copy-start.3
  346.4 3.7 %copy-start.1 = (f32[2,48,1536]{2,1,0:T(8,128)S(1)}, f32[2,48,1536]{2,1,0:T(8,128)}, u32[]{:S(2)}) copy-start(f32[2,48,1536]{2,1,0:T(8,128)} %get-tuple-element.120) | copy-start | bytes 1769476
  346.4 4.5 %copy-start = (f32[2,192,384]{2,1,0:T(8,128)S(1)}, f32[2,192,384]{2,1,0:T(8,128)}, u32[]{:S(2)}) copy-start(f32[2,192,384]{2,1,0:T(8,128)} %get-tuple-element.122) | copy-start | bytes 1769476
